TPU v7x, 512 devices: a whole 4x4x16 slice. The times are simulated.
512 devices in a mesh: tm: 32 (over x_lo, z), space: 16 (over y, x_hi, core).
Axes of the slice: x: 4 (x_hi: 2, x_lo: 2; x = x_hi * 2 + x_lo), y: 4, z: 16, core: 2. Of those that a mesh axis runs over, the one named last changes fastest.
Arguments:
- latents: bfloat16 [64, 32, 160, 256], P('tm', 'space'), may hold values from -6 to 6
- grad_out: bfloat16 [64, 16, 80, 512], P('tm', 'space'), may hold values from -6 to 6
- w_spatial: bfloat16 [2304, 512], P('space'), may hold values from -0.125 to 0.125
- w_temporal: bfloat16 [1536, 512], P('space'), may hold values from -0.15625 to 0.15625
Outputs:
- grad_latents: bfloat16 [64, 32, 160, 256], P('tm', 'space')
- grad_temporal: float32 [1536, 512], P('space')
All inputs are finite; a program needn't handle non-finite values.
Results may differ from a plain program's by a relative error of at most 0.0049.
Values may be sent and summed in bfloat16 or wider, within the bound.
A program may use at most 64 MiB of HBM per device.

v0:
```python
import jax
import jax.numpy as jnp
from jax import lax
from jax.sharding import PartitionSpec as P


def passed_along(value, axis, steps):
    count = lax.axis_size(axis)
    leading, last = (max(0, -steps), min(count, count - steps))
    return lax.ppermute(value, axis, [(source, source + steps) for source in range(leading, last)])


def window_taps(padded, rows_out, cols_out):
    pieces = []
    for row_tap in range(3):
        for col_tap in range(3):
            pieces.append(
                padded[
                    ...,
                    row_tap : row_tap + 2 * rows_out : 2,
                    col_tap : col_tap + 2 * cols_out : 2,
                    :,
                ]
            )
    return jnp.concatenate(pieces, axis=-1)


def column_fold(spread):
    shifted = jnp.concatenate(
        [jnp.zeros_like(spread[..., :1, 2, :]), spread[..., :-1, 2, :]], axis=-2
    )
    even_cols = spread[..., 0, :] + shifted
    paired = jnp.stack([even_cols, spread[..., 1, :]], axis=-2)
    return paired.reshape(paired.shape[:-3] + (2 * paired.shape[-3], paired.shape[-1]))


def spatial_conv(extended, kernel):
    rows_out = (extended.shape[1] - 1) // 2
    cols_out = extended.shape[2] // 2
    padded = jnp.pad(extended, ((0, 0), (0, 0), (0, 1), (0, 0)))
    stacked = window_taps(padded, rows_out, cols_out)
    result = jnp.dot(
        stacked.reshape(-1, stacked.shape[-1]), kernel, preferred_element_type=jnp.float32
    )
    return result.astype(jnp.bfloat16).reshape(
        extended.shape[0], rows_out, cols_out, kernel.shape[1]
    )


def local(latents, grad_out, w_spatial, w_temporal):
    frames, rows_in, cols_in, in_channels = latents.shape
    rows_out = rows_in // 2
    cols_out = cols_in // 2
    channels = grad_out.shape[-1]
    spatial_full, temporal_full = (
        lax.all_gather(w_spatial, "space", axis=0, tiled=True),
        lax.all_gather(w_temporal, "space", axis=0, tiled=True),
    )
    below = passed_along(latents[:, :1], "space", -1)
    extended = jnp.concatenate([latents, below], axis=1)
    activations = spatial_conv(extended, spatial_full)
    previous = passed_along(activations, "tm", 1)
    at_start = lax.axis_index("tm") == 0
    previous = jnp.where(at_start, jnp.stack([activations[0], activations[0]]), previous)
    acts_pad = jnp.concatenate([previous, activations], axis=0)
    following = passed_along(grad_out, "tm", -1)
    grad_pad = jnp.concatenate([grad_out, following], axis=0)
    stacked_acts = jnp.concatenate(
        [acts_pad[tap_index : tap_index + frames] for tap_index in range(3)], axis=-1
    ).reshape(-1, 3 * channels)
    flat_grads = grad_out.reshape(-1, channels)
    share_rows = stacked_acts.shape[1] // lax.axis_size("space")
    full_term = lax.dot_general(
        stacked_acts, flat_grads, (((0,), (0,)), ((), ())), preferred_element_type=jnp.float32
    )
    summed = lax.psum(full_term, ("tm", "space"))
    grad_temporal = lax.dynamic_slice_in_dim(
        summed, lax.axis_index("space") * share_rows, share_rows, 0
    )
    flipped = (
        temporal_full.reshape(3, channels, channels)
        .transpose(0, 2, 1)
        .reshape(3 * channels, channels)
    )
    stacked_grads = jnp.concatenate(
        [grad_pad[2 - tap_index : 2 - tap_index + frames] for tap_index in range(3)], axis=-1
    ).reshape(-1, 3 * channels)
    grad_acts = jnp.dot(stacked_grads, flipped, preferred_element_type=jnp.float32)
    first_grads = grad_out[0].reshape(-1, channels)
    second_grads = grad_out[1].reshape(-1, channels)
    boundary = (
        jnp.dot(first_grads, flipped[:channels], preferred_element_type=jnp.float32)
        + jnp.dot(second_grads, flipped[:channels], preferred_element_type=jnp.float32)
        + jnp.dot(first_grads, flipped[channels : 2 * channels], preferred_element_type=jnp.float32)
    )
    cells = rows_out * cols_out
    correction = jnp.where(at_start, boundary, jnp.zeros_like(boundary))
    grad_acts = jnp.concatenate([grad_acts[:cells] + correction, grad_acts[cells:]], axis=0)
    grad_conv = grad_acts.astype(jnp.bfloat16)
    spread = lax.dot_general(
        grad_conv, spatial_full, (((1,), (1,)), ((), ())), preferred_element_type=jnp.float32
    ).reshape(frames, rows_out, cols_out, 3, 3, in_channels)
    folded = [column_fold(spread[:, :, :, tap_index]) for tap_index in range(3)]
    edge_rows = grad_conv.reshape(frames, rows_out, cols_out, channels)[:, rows_out - 1]
    above = passed_along(edge_rows, "space", 1)
    lower_taps = spatial_full[6 * in_channels :]
    edge_spread = lax.dot_general(
        above.reshape(-1, channels),
        lower_taps,
        (((1,), (1,)), ((), ())),
        preferred_element_type=jnp.float32,
    ).reshape(frames, cols_out, 3, in_channels)
    from_above = column_fold(edge_spread)
    spilled = jnp.concatenate([from_above[:, None], folded[2][:, :-1]], axis=1)
    paired = jnp.stack([folded[0] + spilled, folded[1]], axis=2)
    grad_latents = paired.reshape(frames, rows_in, cols_in, in_channels).astype(jnp.bfloat16)
    return (grad_latents, grad_temporal)


def solution(mesh):
    return jax.shard_map(
        local,
        mesh=mesh,
        in_specs=(
            P("tm", "space", None, None),
            P("tm", "space", None, None),
            P("space", None),
            P("space", None),
        ),
        out_specs=(P("tm", "space", None, None), P("space", None)),
        check_vma=False,
    )
```

profile of v0, /device:TPU:1, one launch (start us, length us, event | category | flops | bytes accessed | tf_op | source)
XLA Modules:
  0.0 654.3 jit_solution(16217405542840735793)
XLA Ops:
  7.2 0.7 all-gather.3.cloned.1.call-update
  7.9 0.7 all-gather.5.cloned.1.call-update
  8.7 0.9 slice.135
  9.6 8.8 %collective-permute-start.2 = (bf16[2,1,160,256]{3,2,1,0:T(8,128)(2,1)S(1)}, bf16[2,1,160,256]{3,2,1,0:T(8,128)(2,1)S(1)}, u32[]{:S(2)}, u32[]{:S(2)}) collective-permute-start(bf16[2,1,160,256]{3,2,1,0:T(8,128)(2,1)S(1)} %slice.135), channel_id=1, source_target_pairs={{1,0},{2,1},{3,2},{4,3},{5,4},{6,5},{7,6},{8,7},{9,8},{10,9},{11,1... | collective-permute-start | bytes 491528 | tf_op jit(solution)/shard_map/ppermute | solution.py:10
  18.4 1.3 collective-permute-start
  19.8 1.1 fusion.4
  20.8 0.1 slice.136
  20.9 0.1 slice.137
  21.1 0.2 slice.138
  21.3 0.1 slice.139
  21.4 0.1 slice.140
  21.5 0.2 slice.141
  22.1 0.2 slice.144
  22.3 4.1 collective-permute-done
  26.5 52.2 %all-gather.3.cloned.1.call-done = bf16[1536,512]{1,0:T(8,128)(2,1)} async-done(((bf16[96,512]{1,0:T(8,128)(2,1)}), bf16[1536,512]{1,0:T(8,128)(2,1)}) %all-gather.3.cloned.1.call-update) | async-done | bytes 1572880 | tf_op jit(solution)/shard_map/all_gather | solution.py:57
  78.7 1.7 copy.28
  80.4 0.4 fusion.34
  80.9 1.0 copy-done.1
  81.8 0.3 fusion.14
  82.1 0.3 convolution_add_fusion.1
  82.4 0.3 fusion.1
  82.7 0.7 maximum_convert_fusion
  83.4 2.3 collective-permute-start.1
  85.7 59.0 %all-gather.5.cloned.1.call-done = bf16[2304,512]{1,0:T(8,128)(2,1)} async-done(((bf16[144,512]{1,0:T(8,128)(2,1)}), bf16[2304,512]{1,0:T(8,128)(2,1)}) %all-gather.5.cloned.1.call-update) | async-done | bytes 2359312 | tf_op jit(solution)/shard_map/all_gather | solution.py:56
  144.7 2.6 fusion.33
  147.2 1.8 reshape.70
  149.0 1.7 slice_bitcast_fusion.1
  150.7 0.2 slice_bitcast_fusion.11
  150.9 0.2 slice_bitcast_fusion.12
  151.1 0.2 copy-done.5
  151.3 0.5 convolution_convert_fusion
  151.8 3.2 collective-permute-start.3
  155.0 3.3 collective-permute-done.3
  158.4 2.3 convolution_bitcast_fusion
  160.7 1.5 fusion.18
  162.2 1.3 slice.207
  163.4 0.2 slice.155
  163.6 0.4 pad_maximum_fusion.4
  164.0 0.2 copy.44
  164.2 1.3 fusion.23
  165.6 0.3 copy.33
  165.9 0.3 pad_maximum_fusion.2
  166.2 0.3 copy.43
  166.5 0.2 fusion.15
  166.7 0.5 maximum_bitcast_fusion
  167.1 0.8 copy.41
  167.9 478.3 %all-reduce.6.cloned.1.call-done = f32[1536,512]{1,0:T(8,128)} async-done(((f32[1536,512]{1,0:T(8,128)}), f32[1536,512]{1,0:T(8,128)}) %all-reduce.6.cloned.1.call-update) | async-done | bytes 3145744 | tf_op jit(solution)/shard_map/psum | solution.py:76
  646.2 1.6 constant_dynamic-slice_fusion
  (37 shorter events, 0.7 us)
Async XLA Ops:
  7.2 71.5 %all-gather.3.cloned.1.call-start = ((), (), s32[]{:S(2)}) async-start(), calls=%async_computation | async-start | bytes 1671168 | tf_op jit(solution)/shard_map/all_gather | solution.py:57
  7.9 136.8 %all-gather.5.cloned.1.call-start = ((), (), s32[]{:S(2)}) async-start(), calls=%async_computation.1 | async-start | bytes 2506752 | tf_op jit(solution)/shard_map/all_gather | solution.py:56
  8.6 637.6 %all-reduce.6.cloned.1.call-start = ((), (), s32[]{:S(2)}) async-start(), calls=%async_computation.2 | async-start | bytes 6291456 | tf_op jit(solution)/shard_map/psum | solution.py:76
  9.6 10.1 %collective-permute-start.2 = (bf16[2,1,160,256]{3,2,1,0:T(8,128)(2,1)S(1)}, bf16[2,1,160,256]{3,2,1,0:T(8,128)(2,1)S(1)}, u32[]{:S(2)}, u32[]{:S(2)}) collective-permute-start(bf16[2,1,160,256]{3,2,1,0:T(8,128)(2,1)S(1)} %slice.135), channel_id=1, source_target_pairs={{1,0},{2,1},{3,2},{4,3},{5,4},{6,5},{7,6},{8,7},{9,8},{10,9},{11,1... | collective-permute-start | bytes 491528 | tf_op jit(solution)/shard_map/ppermute | solution.py:10
  18.4 8.0 %collective-permute-start = (bf16[2,1,80,512]{3,2,1,0:T(8,128)(2,1)}, bf16[2,1,80,512]{3,2,1,0:T(8,128)(2,1)S(1)}, u32[]{:S(2)}, u32[]{:S(2)}) collective-permute-start(bf16[2,1,80,512]{3,2,1,0:T(8,128)(2,1)} %param.5), channel_id=1, source_target_pairs={{16,0},{32,16},{48,32},{64,48},{80,64},{96,80},{112,96},{128,112},... | collective-permute-start | bytes 491528 | tf_op jit(solution)/shard_map/ppermute | solution.py:10
  19.7 6.7 %copy-start.2 = (bf16[2,1,80,512]{3,2,1,0:T(8,128)(2,1)S(1)}, bf16[2,1,80,512]{3,2,1,0:T(8,128)(2,1)}, u32[]{:S(2)}) copy-start(bf16[2,1,80,512]{3,2,1,0:T(8,128)(2,1)} %param.5) | copy-start | bytes 491524
  22.3 56.4 %copy-start.4 = (bf16[2,1,80,2304]{3,2,1,0:T(8,128)(2,1)}, bf16[2,1,80,2304]{3,2,1,0:T(8,128)(2,1)S(1)}, u32[]{:S(2)}) copy-start(bf16[2,1,80,2304]{3,2,1,0:T(8,128)(2,1)S(1)} %constant_dynamic-update-slice_fusion) | copy-start | bytes 2211844
  80.4 1.4 copy-start.1
  83.4 80.8 %collective-permute-start.1 = (bf16[2,80,512]{2,1,0:T(8,128)(2,1)}, bf16[2,80,512]{2,1,0:T(8,128)(2,1)}, u32[]{:S(2)}, u32[]{:S(2)}) collective-permute-start(bf16[2,80,512]{2,1,0:T(8,128)(2,1)} %bitcast.14), channel_id=1, source_target_pairs={{0,1},{1,2},{2,3},{3,4},{4,5},{5,6},{6,7},{7,8},{8,9},{9,10},{10,1... | collective-permute-start | bytes 491528 | tf_op jit(solution)/shard_map/ppermute | solution.py:10
  149.0 2.1 copy-start
  149.0 2.2 copy-start.5
  150.7 4.3 copy-start.3
  151.8 6.5 collective-permute-start.3
  160.7 3.5 slice-start
Sparse Core Ops, SparseCore 0:
  11.3 67.2 all-gather.2
  82.0 62.5 all-gather.4
  160.8 485.3 all-reduce.5
where the time goes:
time: 655 us; the launch traced here: 654 us
  waiting for transfers between devices  598 us (91%)
  starting transfers between devices  15.7 us (2%)
  between operations  14.2 us (2%)
  local copies, waits for them, and re-layouts  13.5 us (2%)
  matrix products  8.02 us (1%)
    psum x1, waiting for transfers between devices, local(): summed = lax.psum(full_term, ('tm', 'space'))  478 us
    all_gather x1, waiting for transfers between devices, local(): lax.all_gather(w_spatial, 'space', axis=0, tiled=True)  59 us
    all_gather x1, waiting for transfers between devices, local(): lax.all_gather(w_temporal, 'space', axis=0, tiled=True)  52.2 us
    ppermute x4, starting transfers between devices, passed_along(): lax.ppermute(value, axis, [(source, source + steps) for source in range(l...  15.6 us
  transfers between devices with their start and end apart: 7, of which 5 were waited for; matrix products, arithmetic and copies ran while one was open for 4% of the time, Pallas kernels for 0%

commit v1 on v0

v1 whole, which is shorter than its diff:
```python
import jax
import jax.numpy as jnp
from jax import lax
from jax.experimental import pallas as pl
from jax.experimental.pallas import tpu as pltpu
from jax.sharding import PartitionSpec as P

MESH = pl.DeviceIdType.MESH
F32 = jnp.float32
BF16 = jnp.bfloat16
SUBS = 2
ARRIVAL = (4, 1, 3, 5, 7, 2, 6)
RELAY = {4: 0, 1: 1, 3: 2, 5: 0, 7: 1, 2: 2, 6: 0}


def dot(a, b, ca, cb):
    return lax.dot_general(a, b, (((ca,), (cb,)), ((), ())), preferred_element_type=F32)


def place(x, y, z, c):
    return (lax.rem(x, 2) * 16 + z, y * 4 + (x // 2) * 2 + c)


def kernel(
    lat_hbm, gout_hbm, ws_hbm, wt_hbm, out_hbm, gt_hbm,
    lat, ws, wt, grads, eo, wide, patches, acts, tsum, tsend, trecv, zbuf,
    fin, fout, gap, gap_in, ga, shifted, po, po_in, outv,
    loc_sem, pair_s, pair_r, ext_s, ext_r, rel_s, rel_r, halo_s, halo_r,
    rs_s, rs_r, z_s, z_r, fin_s, fin_r,
):
    tm, sp = lax.axis_index("tm"), lax.axis_index("space")
    xl, z = tm // 16, lax.rem(tm, 16)
    c, chip = lax.rem(sp, 2), sp // 2
    y, xh = chip // 2, lax.rem(chip, 2)
    x = 2 * xh + xl
    par = lax.rem(xl + xh + z, 2)
    other = 1 - c
    z_up, z_down = lax.rem(z + 1, 16), lax.rem(z + 15, 16)

    partner = place(x, y, z, other)
    ups = [place(x, y, z_up, c), place(x, y, z_down, c), place(jnp.bitwise_xor(x, 1), y, z, c)]
    final_to = place(jnp.bitwise_xor(x, 1), y, z, xl)
    plane = []
    for dy in range(4):
        for dx in range(4):
            if dx or dy:
                plane.append((lax.rem(x + dx, 4), lax.rem(y + dy, 4)))
    tm_next, tm_prev = lax.rem(tm + 1, 32), lax.rem(tm + 31, 32)

    def half(index):
        return pl.ds(pl.multiple_of(index * 256, 256), 256)

    def rows(index, count):
        return pl.ds(pl.multiple_of(index * count, count), count)

    loads = [
        pltpu.make_async_copy(ws_hbm.at[:, half(c)], ws.at[rows(sp, 144)], loc_sem.at[0]),
        pltpu.make_async_copy(wt_hbm.at[:, half(c)], wt.at[rows(sp, 96)], loc_sem.at[1]),
        pltpu.make_async_copy(lat_hbm, lat, loc_sem.at[2]),
        pltpu.make_async_copy(gout_hbm.at[:, 0, :, half(c)], grads.at[pl.ds(0, 2), c], loc_sem.at[3]),
    ]
    for copy in loads:
        copy.start()

    barrier = pltpu.get_barrier_semaphore()
    greeted = [partner, ups[0], ups[1], place(jnp.bitwise_xor(x, 1), y, z, other), (tm_next, sp), (tm_next, chip * 2 + other)]
    greeted += [place(px, py, z, c) for px, py in plane]
    for device in greeted:
        pl.semaphore_signal(barrier, inc=1, device_id=device, device_id_type=MESH)
    pl.semaphore_wait(barrier, len(greeted))

    sent = []

    def send(src, dst, ssem, rsem, device):
        copy = pltpu.make_async_remote_copy(
            src_ref=src, dst_ref=dst, send_sem=ssem, recv_sem=rsem, device_id=device, device_id_type=MESH
        )
        copy.start()
        return copy

    pair_ws = send(ws_hbm.at[:, half(other)], ws.at[rows(sp, 144)], pair_s.at[0], pair_r.at[0], partner)
    pair_wt = send(wt_hbm.at[:, half(other)], wt.at[rows(sp, 96)], pair_s.at[1], pair_r.at[1], partner)
    pair_g = send(
        gout_hbm.at[:, 0, :, half(other)], grads.at[pl.ds(0, 2), c], pair_s.at[2], pair_r.at[2], partner
    )
    sent += [pair_ws, pair_wt, pair_g]

    def piece_chip(r):
        dxo, dy = r // 4, r % 4
        return lax.rem(y + 4 - dy, 4) * 2 + jnp.bitwise_xor(xh, dxo)

    def ext_device(r):
        dxo, dy = r // 4, r % 4
        tx = 3 - x if dxo else x
        return place(tx, lax.rem(y + dy, 4), z, c)

    mine = chip * 2 + par
    weights = ((ws, 144, 0), (wt, 96, 1))

    def ext_send(which):
        buf, count, lane = weights[which]
        return [
            send(buf.at[rows(mine, count)], buf.at[rows(mine, count)], ext_s.at[lane, r], ext_r.at[lane, r], ext_device(r))
            for r in ARRIVAL
        ]

    loads[0].wait()
    pair_ws.wait_recv()
    ext_ws = ext_send(0)
    loads[1].wait()
    pair_wt.wait_recv()
    ext_wt = ext_send(1)
    sent += ext_ws + ext_wt

    halo = []
    for h in range(2):
        halo.append(
            pltpu.make_async_remote_copy(
                src_ref=gout_hbm.at[:, 0, :, pl.ds(256 * h, 256)],
                dst_ref=grads.at[pl.ds(2, 2), c],
                send_sem=halo_s.at[h],
                recv_sem=halo_r.at[c],
                device_id=(tm_prev, chip * 2 + h),
                device_id_type=MESH,
            )
        )

    @pl.when(tm > 0)
    def _():
        for copy in halo:
            copy.start()

    loads[2].wait()
    for f in range(2):
        for r in range(2):
            for lane in range(2):
                across = pl.ds(128 * lane, 128)
                wide[lane] = lat[f, r, :, across].astype(F32)
                for odd in range(2):
                    eo[2 * c + r, f, odd, :, across] = wide[lane, pl.ds(odd, 80, 2), :].astype(BF16)
    pair_eo = send(eo.at[pl.ds(2 * c, 2)], eo.at[pl.ds(2 * c, 2)], pair_s.at[3], pair_r.at[3], partner)
    sent.append(pair_eo)
    pair_eo.wait_recv()

    prev_chip = lax.rem(chip + 7, 8)
    next_chip = lax.rem(chip + 1, 8)
    row_up = pltpu.make_async_remote_copy(
        src_ref=eo.at[0],
        dst_ref=eo.at[4],
        send_sem=halo_s.at[2],
        recv_sem=halo_r.at[2],
        device_id=(tm, prev_chip * 2 + c),
        device_id_type=MESH,
    )

    @pl.when(chip > 0)
    def _():
        row_up.start()

    @pl.when(chip == 7)
    def _():
        eo[4] = jnp.zeros_like(eo[4])

    @pl.when(tm == 31)
    def _():
        grads[2:4] = jnp.zeros_like(grads[2:4])

    last = lax.broadcasted_iota(jnp.int32, (80, 256), 0) == 79
    first = lax.broadcasted_iota(jnp.int32, (80, 256), 0) == 0

    def place_patch(f, i, r):
        row = 2 * i + r
        block = pl.ds((f * 2 + i) * 80, 80)
        even = eo[row, f, 0]
        moved = jnp.where(last, 0.0, pltpu.roll(even.astype(F32), 79, 0)).astype(BF16)
        patches[block, pl.ds(3 * r * 256, 256)] = even
        patches[block, pl.ds((3 * r + 1) * 256, 256)] = eo[row, f, 1]
        patches[block, pl.ds((3 * r + 2) * 256, 256)] = moved

    for f in range(2):
        for i in range(2):
            for r in range(3):
                if 2 * i + r < 4:
                    place_patch(f, i, r)

    def relay(which):
        buf, count, lane = weights[which]
        copies = []
        for at, r in enumerate(ARRIVAL):
            (ext_ws, ext_wt)[which][at].wait_recv()
            index = piece_chip(r) * 2 + par
            copies.append(
                send(buf.at[rows(index, count)], buf.at[rows(index, count)], rel_s.at[lane, r], rel_r.at[lane, r], ups[RELAY[r]])
            )
        return copies

    rel_ws = relay(0)

    @pl.when(chip < 7)
    def _():
        row_up.wait_recv()

    for f in range(2):
        place_patch(f, 1, 2)
    for copy in rel_ws:
        copy.wait_recv()

    acts[c] = jnp.dot(patches[...], ws[...], preferred_element_type=F32).astype(BF16)
    pair_a = send(acts.at[c], acts.at[c], pair_s.at[4], pair_r.at[4], partner)
    rel_wt = relay(1)
    sent += rel_ws + rel_wt + [pair_a]

    loads[3].wait()
    pair_g.wait_recv()

    @pl.when(tm < 31)
    def _():
        for core in range(2):
            pltpu.make_async_copy(grads.at[pl.ds(2, 2), core], grads.at[pl.ds(2, 2), core], halo_r.at[core]).wait()

    pair_a.wait_recv()

    def frames(start, count):
        return grads[start : start + count].reshape(count * 160, 256)

    for k in range(3):
        for h in range(2):
            tsum[pl.ds(k * 512 + h * 256, 256)] = dot(acts[h], frames(2 - k, 2), 0, 0)

    @pl.when(tm == 0)
    def _():
        for h in range(2):
            first_acts = acts[h, 0:160]
            zero = dot(first_acts, frames(0, 1), 0, 0)
            tsum[pl.ds(h * 256, 256)] += zero + dot(first_acts, frames(1, 1), 0, 0)
            tsum[pl.ds(512 + h * 256, 256)] += zero

    tsend[...] = tsum[...].astype(BF16)
    spread = []
    for at, (px, py) in enumerate(plane):
        block = 4 * py + px
        spread.append(
            send(tsend.at[rows(block, 96)], trecv.at[at], rs_s.at[at], rs_r.at[at], place(px, py, z, c))
        )
    sent += spread

    for copy in rel_wt:
        copy.wait_recv()
    for h in range(2):
        total = dot(frames(2, 2), wt[pl.ds(h * 256, 256)], 1, 1)
        total += dot(frames(1, 2), wt[pl.ds(512 + h * 256, 256)], 1, 1)
        total += dot(frames(0, 2), wt[pl.ds(1024 + h * 256, 256)], 1, 1)
        gap[h] = total

    @pl.when(tm == 0)
    def _():
        for h in range(2):
            more = dot(frames(0, 1), wt[pl.ds(h * 256, 256)], 1, 1)
            more += dot(frames(1, 1), wt[pl.ds(h * 256, 256)], 1, 1)
            more += dot(frames(0, 1), wt[pl.ds(512 + h * 256, 256)], 1, 1)
            gap[h, 0:160] += more

    pair_p = send(gap.at[other], gap_in, pair_s.at[5], pair_r.at[5], partner)
    sent.append(pair_p)
    pair_p.wait_recv()
    for f in range(2):
        for i in range(2):
            block = pl.ds((f * 2 + i) * 80, 80)
            ga[1 + i, f] = (gap[c, block] + gap_in[block]).astype(BF16)
    row_down = pltpu.make_async_remote_copy(
        src_ref=ga.at[2],
        dst_ref=ga.at[0],
        send_sem=halo_s.at[3],
        recv_sem=halo_r.at[3],
        device_id=(tm, next_chip * 2 + c),
        device_id_type=MESH,
    )

    @pl.when(chip < 7)
    def _():
        row_down.start()

    for copy in spread:
        copy.wait_recv()
    own_block = tsend[rows(4 * y + x, 96)].astype(F32)
    for at in range(15):
        own_block += trecv[at].astype(F32)
    zbuf[z] = own_block.astype(BF16)
    step_rows = 96 // SUBS
    ring = {}

    def ring_send(step, way, part):
        origin = lax.rem(z + 16 + (-(step - 1) if way == 0 else step - 1), 16)
        ref = zbuf.at[origin, pl.ds(part * step_rows, step_rows)]
        ring[step, way, part] = send(ref, ref, z_s.at[step, way, part], z_r.at[step, way, part], ups[way])

    def parts(step, way):
        if step < 8:
            return range(SUBS)
        return range(SUBS // 2) if way == 0 else range(SUBS // 2, SUBS)

    for part in range(SUBS):
        for way in range(2):
            ring_send(1, way, part)

    @pl.when(chip == 0)
    def _():
        ga[0] = jnp.zeros_like(ga[0])

    @pl.when(chip > 0)
    def _():
        row_down.wait_recv()

    def ring_step(step):
        for part in range(SUBS):
            for way in range(2):
                ring[step - 1, way, part].wait_recv()
                if part in parts(step, way):
                    ring_send(step, way, part)

    for row in range(3):
        for f in range(2):
            moved = jnp.where(first, 0.0, pltpu.roll(ga[row, f].astype(F32), 1, 0))
            shifted[row, f] = moved.astype(BF16)

    def tap(r, s):
        return ws[pl.ds((3 * r + s) * 256, 256)]

    cur, prev = ga[1:3].reshape(320, 256), ga[0:2].reshape(320, 256)
    cur_s, prev_s = shifted[1:3].reshape(320, 256), shifted[0:2].reshape(320, 256)

    def put(kind, value):
        po[0, kind] = value[:160]
        po[1, kind] = value[160:]

    ring_step(2)
    put(0, dot(cur, tap(0, 0), 1, 1) + dot(cur_s, tap(0, 2), 1, 1) + dot(prev, tap(2, 0), 1, 1) + dot(prev_s, tap(2, 2), 1, 1))
    ring_step(3)
    put(1, dot(cur, tap(0, 1), 1, 1) + dot(prev, tap(2, 1), 1, 1))
    ring_step(4)
    put(2, dot(cur, tap(1, 0), 1, 1) + dot(cur_s, tap(1, 2), 1, 1))
    put(3, dot(cur, tap(1, 1), 1, 1))
    pair_o = send(po.at[other], po_in, pair_s.at[6], pair_r.at[6], partner)
    sent.append(pair_o)
    ring_step(5)
    pair_o.wait_recv()

    def finish(f, r):
        block = pl.ds(f * 80, 80)
        for lane in range(2):
            across = pl.ds(128 * lane, 128)
            for odd in range(2):
                kind = 2 * r + odd
                wide[lane, pl.ds(odd, 80, 2), :] = po[c, kind, block, across] + po_in[kind, block, across]
            outv[f, r, :, across] = wide[lane].astype(BF16)

    finish(0, 0)
    finish(0, 1)
    ring_step(6)
    finish(1, 0)
    finish(1, 1)
    write_out = pltpu.make_async_copy(outv, out_hbm, loc_sem.at[4])
    write_out.start()
    ring_step(7)
    ring_step(8)
    for way in range(2):
        for part in parts(8, way):
            ring[8, way, part].wait_recv()
    sent += list(ring.values())
    total = zbuf[0].astype(F32)
    for at in range(1, 16):
        total += zbuf[at].astype(F32)
    fin[...] = total

    far = pltpu.make_async_remote_copy(
        src_ref=fin, dst_ref=fout.at[c], send_sem=fin_s.at[0], recv_sem=fin_r.at[c], device_id=final_to, device_id_type=MESH
    )
    near = pltpu.make_async_remote_copy(
        src_ref=fin, dst_ref=fout.at[c], send_sem=fin_s.at[1], recv_sem=fin_r.at[c], device_id=partner, device_id_type=MESH
    )
    far.start()

    def landed(h):
        pltpu.make_async_copy(fout.at[h], fout.at[h], fin_r.at[h]).wait()

    @pl.when(c == xl)
    def _():
        fout[c] = fin[...]
        landed(other)

    @pl.when(c != xl)
    def _():
        near.start()
        landed(0)
        landed(1)
        near.wait_send()

    writes = [
        pltpu.make_async_copy(fout.at[h], gt_hbm.at[:, pl.ds(256 * h, 256)], loc_sem.at[5 + h]) for h in range(2)
    ]
    for copy in writes:
        copy.start()
    far.wait_send()
    for copy in sent:
        copy.wait_send()

    @pl.when(tm > 0)
    def _():
        for copy in halo:
            copy.wait_send()

    @pl.when(chip > 0)
    def _():
        row_up.wait_send()

    @pl.when(chip < 7)
    def _():
        row_down.wait_send()

    write_out.wait()
    for copy in writes:
        copy.wait()


def local(latents, grad_out, w_spatial, w_temporal):
    dma = pltpu.SemaphoreType.DMA
    vmem = pltpu.VMEM
    return pl.pallas_call(
        kernel,
        out_shape=(
            jax.ShapeDtypeStruct(latents.shape, BF16),
            jax.ShapeDtypeStruct((96, 512), F32),
        ),
        in_specs=[pl.BlockSpec(memory_space=pl.ANY)] * 4,
        out_specs=[pl.BlockSpec(memory_space=pl.ANY)] * 2,
        scratch_shapes=[
            vmem((2, 2, 160, 256), BF16),
            vmem((2304, 256), BF16),
            vmem((1536, 256), BF16),
            vmem((4, 2, 80, 256), BF16),
            vmem((5, 2, 2, 80, 256), BF16),
            vmem((2, 160, 128), F32),
            vmem((320, 2304), BF16),
            vmem((2, 320, 256), BF16),
            vmem((1536, 256), F32),
            vmem((1536, 256), BF16),
            vmem((15, 96, 256), BF16),
            vmem((16, 96, 256), BF16),
            vmem((96, 256), F32),
            vmem((2, 96, 256), F32),
            vmem((2, 320, 256), F32),
            vmem((320, 256), F32),
            vmem((3, 2, 80, 256), BF16),
            vmem((3, 2, 80, 256), BF16),
            vmem((2, 4, 160, 256), F32),
            vmem((4, 160, 256), F32),
            vmem((2, 2, 160, 256), BF16),
            dma((7,)),
            dma((7,)),
            dma((7,)),
            dma((2, 8)),
            dma((2, 8)),
            dma((2, 8)),
            dma((2, 8)),
            dma((4,)),
            dma((4,)),
            dma((15,)),
            dma((15,)),
            dma((9, 2, SUBS)),
            dma((9, 2, SUBS)),
            dma((2,)),
            dma((2,)),
        ],
        compiler_params=pltpu.CompilerParams(
            collective_id=0, has_side_effects=True, vmem_limit_bytes=48 * 2**20
        ),
    )(latents, grad_out, w_spatial, w_temporal)


def solution(mesh):
    return jax.shard_map(
        local,
        mesh=mesh,
        in_specs=(
            P("tm", "space", None, None),
            P("tm", "space", None, None),
            P("space", None),
            P("space", None),
        ),
        out_specs=(P("tm", "space", None, None), P("space", None)),
        check_vma=False,
    )
```

time: 655 us -> 86.3 us (0.13)
  waiting for transfers between devices: 598 us -> 0 us
  Pallas kernels: 0 us -> 80.3 us
  starting transfers between devices: 15.7 us -> 0 us
  between operations: 14.2 us -> 0.65 us
  local copies, waits for them, and re-layouts: 13.5 us -> 5.09 us
  matrix products: 8.02 us -> 0 us
    psum x1 -> x0, waiting for transfers between devices: 478 us -> none  [local(): summed = lax.psum(full_term, ('tm', 'space'))]
    all_gather x2 -> x0, waiting for transfers between devices: 111 us -> none  [the longest x1 59 us: local(): lax.all_gather(w_spatial, 'space', axis=0, tiled=True)]
    pallas_call x0 -> x1, Pallas kernels: none -> 80.3 us  [local(): pl.pallas_call(kernel, out_shape=(jax.ShapeDtypeStruct(latents.shape, BF1...]
    ppermute x4 -> x0, starting transfers between devices: 15.6 us -> none  [passed_along(): lax.ppermute(value, axis, [(source, source + steps) for source in range(l...]
    dot_general x8 -> x0, matrix products: 8.02 us -> none  [the longest x1 2.58 us: local(): lax.dot_general(grad_conv, spatial_full, (((1,), (1,)), ((), ())), prefer...]
    ppermute x4 -> x0, waiting for transfers between devices: 7.43 us -> none  [passed_along(): lax.ppermute(value, axis, [(source, source + steps) for source in range(l...]
  transfers between devices with their start and end apart: 7 -> 0, of which waited for: 5 -> 0; matrix products, arithmetic and copies ran while one was open for 4% -> 0% of each run, Pallas kernels for 0% -> 0%
where the time goes in v1:
time: 86.3 us; the launch traced here: 86 us
  Pallas kernels  80.3 us (93%)
  local copies, waits for them, and re-layouts  5.09 us (6%)
    pallas_call x1, Pallas kernels, local(): pl.pallas_call(kernel, out_shape=(jax.ShapeDtypeStruct(latents.shape, BF1...  80.3 us
    unnamed x10, local copies, waits for them, and re-layouts  5.09 us

profile of v1, /device:TPU:1, one launch (start us, length us, event | category | flops | bytes accessed | tf_op | source)
XLA Modules:
  0.0 86.0 jit_solution(5421144753631605863)
XLA Ops:
  0.6 0.0 copy-start
  0.6 1.0 %copy-done = bf16[2,2,160,256]{3,2,1,0:T(8,128)(2,1)S(1)} copy-done((bf16[2,2,160,256]{3,2,1,0:T(8,128)(2,1)S(1)}, bf16[2,2,160,256]{3,2,1,0:T(8,128)(2,1)}, u32[]{:S(2)}) %copy-start) | copy-done | bytes 327704
  1.6 0.0 copy-start.1
  1.6 0.9 %copy-done.1 = bf16[2,1,80,512]{3,2,1,0:T(8,128)(2,1)S(1)} copy-done((bf16[2,1,80,512]{3,2,1,0:T(8,128)(2,1)S(1)}, bf16[2,1,80,512]{3,2,1,0:T(8,128)(2,1)}, u32[]{:S(2)}) %copy-start.1) | copy-done | bytes 163864
  2.5 0.0 copy-start.2
  2.5 0.9 %copy-done.2 = bf16[144,512]{1,0:T(8,128)(2,1)S(1)} copy-done((bf16[144,512]{1,0:T(8,128)(2,1)S(1)}, bf16[144,512]{1,0:T(8,128)(2,1)}, u32[]{:S(2)}) %copy-start.2) | copy-done | bytes 147480
  3.4 0.0 copy-start.3
  3.4 0.9 %copy-done.3 = bf16[96,512]{1,0:T(8,128)(2,1)S(1)} copy-done((bf16[96,512]{1,0:T(8,128)(2,1)S(1)}, bf16[96,512]{1,0:T(8,128)(2,1)}, u32[]{:S(2)}) %copy-start.3) | copy-done | bytes 98328
  4.3 80.3 %shard_map.59 = (bf16[2,2,160,256]{3,2,1,0:T(8,128)(2,1)S(1)}, f32[96,512]{1,0:T(8,128)S(1)}) custom-call(bf16[2,2,160,256]{3,2,1,0:T(8,128)(2,1)S(1)} %copy-done, bf16[2,1,80,512]{3,2,1,0:T(8,128)(2,1)S(1)} %copy-done.1, bf16[144,512]{1,0:T(8,128)(2,1)S(1)} %copy-done.2, bf16[96,512]{1,0:T(8,128)(2,1)S(1)} %copy-done.3), custom_call_target="tpu_custom_call" | custom-call | tf_op jit(solution)/shard_map/pallas_call | solution.py:428
  84.6 0.7 copy.8
  85.4 0.7 copy.9
Async XLA Ops:
  0.6 1.0 %copy-start = (bf16[2,2,160,256]{3,2,1,0:T(8,128)(2,1)S(1)}, bf16[2,2,160,256]{3,2,1,0:T(8,128)(2,1)}, u32[]{:S(2)}) copy-start(bf16[2,2,160,256]{3,2,1,0:T(8,128)(2,1)} %lat_hbm.1) | copy-start | bytes 983044
  1.6 0.9 %copy-start.1 = (bf16[2,1,80,512]{3,2,1,0:T(8,128)(2,1)S(1)}, bf16[2,1,80,512]{3,2,1,0:T(8,128)(2,1)}, u32[]{:S(2)}) copy-start(bf16[2,1,80,512]{3,2,1,0:T(8,128)(2,1)} %gout_hbm.1) | copy-start | bytes 491524
  2.5 0.9 %copy-start.2 = (bf16[144,512]{1,0:T(8,128)(2,1)S(1)}, bf16[144,512]{1,0:T(8,128)(2,1)}, u32[]{:S(2)}) copy-start(bf16[144,512]{1,0:T(8,128)(2,1)} %ws_hbm.1) | copy-start | bytes 442372
  3.4 0.9 %copy-start.3 = (bf16[96,512]{1,0:T(8,128)(2,1)S(1)}, bf16[96,512]{1,0:T(8,128)(2,1)}, u32[]{:S(2)}) copy-start(bf16[96,512]{1,0:T(8,128)(2,1)} %wt_hbm.1) | copy-start | bytes 294916

commit v2 on v1

--- a/solution.py
+++ b/solution.py
@@ -8,7 +8,6 @@
 MESH = pl.DeviceIdType.MESH
 F32 = jnp.float32
 BF16 = jnp.bfloat16
-SUBS = 2
 ARRIVAL = (4, 1, 3, 5, 7, 2, 6)
 RELAY = {4: 0, 1: 1, 3: 2, 5: 0, 7: 1, 2: 2, 6: 0}
 
@@ -22,11 +21,11 @@
 
 
 def kernel(
-    lat_hbm, gout_hbm, ws_hbm, wt_hbm, out_hbm, gt_hbm,
-    lat, ws, wt, grads, eo, wide, patches, acts, tsum, tsend, trecv, zbuf,
-    fin, fout, gap, gap_in, ga, shifted, po, po_in, outv,
+    lat_hbm, gout_hbm, ws_hbm, wt_hbm, outv, gt,
+    lat, ws, wt, grads, eo, wide, patches, acts, tsum, tsend, trecv,
+    near, near_in, far, quad, fout, gap, gap_in, ga, shifted, po, po_in,
     loc_sem, pair_s, pair_r, ext_s, ext_r, rel_s, rel_r, halo_s, halo_r,
-    rs_s, rs_r, z_s, z_r, fin_s, fin_r,
+    rs_s, rs_r, near_s, near_r, far_s, far_r, fin_s, fin_r, known,
 ):
     tm, sp = lax.axis_index("tm"), lax.axis_index("space")
     xl, z = tm // 16, lax.rem(tm, 16)
@@ -39,7 +38,7 @@
 
     partner = place(x, y, z, other)
     ups = [place(x, y, z_up, c), place(x, y, z_down, c), place(jnp.bitwise_xor(x, 1), y, z, c)]
-    final_to = place(jnp.bitwise_xor(x, 1), y, z, xl)
+    zq, zr = z // 4, lax.rem(z, 4)
     plane = []
     for dy in range(4):
         for dx in range(4):
@@ -69,6 +68,15 @@
         pl.semaphore_signal(barrier, inc=1, device_id=device, device_id_type=MESH)
     pl.semaphore_wait(barrier, len(greeted))
 
+    def meet(stage):
+        for way in (1, -1):
+            there = place(x, y, lax.rem(z + 16 + way * 2**stage, 16), c)
+            pl.semaphore_signal(known.at[stage], inc=1, device_id=there, device_id_type=MESH)
+
+    def met(stage):
+        pl.semaphore_wait(known.at[stage], 2)
+
+    meet(0)
     sent = []
 
     def send(src, dst, ssem, rsem, device):
@@ -107,10 +115,7 @@
     loads[0].wait()
     pair_ws.wait_recv()
     ext_ws = ext_send(0)
-    loads[1].wait()
-    pair_wt.wait_recv()
-    ext_wt = ext_send(1)
-    sent += ext_ws + ext_wt
+    sent += ext_ws
 
     halo = []
     for h in range(2):
@@ -130,6 +135,9 @@
         for copy in halo:
             copy.start()
 
+    met(0)
+    meet(1)
+
     loads[2].wait()
     for f in range(2):
         for r in range(2):
@@ -183,18 +191,25 @@
                 if 2 * i + r < 4:
                     place_patch(f, i, r)
 
-    def relay(which):
+    met(1)
+    meet(2)
+
+    def relay(which, arriving):
         buf, count, lane = weights[which]
         copies = []
         for at, r in enumerate(ARRIVAL):
-            (ext_ws, ext_wt)[which][at].wait_recv()
+            arriving[at].wait_recv()
             index = piece_chip(r) * 2 + par
             copies.append(
                 send(buf.at[rows(index, count)], buf.at[rows(index, count)], rel_s.at[lane, r], rel_r.at[lane, r], ups[RELAY[r]])
             )
         return copies
 
-    rel_ws = relay(0)
+    rel_ws = relay(0, ext_ws)
+    loads[1].wait()
+    pair_wt.wait_recv()
+    ext_wt = ext_send(1)
+    sent += rel_ws + ext_wt
 
     @pl.when(chip < 7)
     def _():
@@ -207,8 +222,7 @@
 
     acts[c] = jnp.dot(patches[...], ws[...], preferred_element_type=F32).astype(BF16)
     pair_a = send(acts.at[c], acts.at[c], pair_s.at[4], pair_r.at[4], partner)
-    rel_wt = relay(1)
-    sent += rel_ws + rel_wt + [pair_a]
+    sent.append(pair_a)
 
     loads[3].wait()
     pair_g.wait_recv()
@@ -244,6 +258,8 @@
         )
     sent += spread
 
+    rel_wt = relay(1, ext_wt)
+    sent += rel_wt
     for copy in rel_wt:
         copy.wait_recv()
     for h in range(2):
@@ -262,6 +278,23 @@
 
     pair_p = send(gap.at[other], gap_in, pair_s.at[5], pair_r.at[5], partner)
     sent.append(pair_p)
+
+    for copy in spread:
+        copy.wait_recv()
+    block_sum = tsend[rows(4 * y + x, 96)].astype(F32)
+    for at in range(15):
+        block_sum += trecv[at].astype(F32)
+    for q in range(4):
+        near[q] = block_sum[48 * (q // 2) : 48 * (q // 2) + 48, 128 * (q % 2) : 128 * (q % 2) + 128].astype(BF16)
+    near_copies = []
+    for j in range(1, 4):
+        to = lax.rem(zr + j, 4)
+        near_copies.append(
+            send(near.at[to], near_in.at[zr], near_s.at[j], near_r.at[j], place(x, y, 4 * zq + to, c))
+        )
+    sent += near_copies
+    near_in[zr] = near[zr]
+
     pair_p.wait_recv()
     for f in range(2):
         for i in range(2):
@@ -280,28 +313,20 @@
     def _():
         row_down.start()
 
-    for copy in spread:
+    for copy in near_copies:
         copy.wait_recv()
-    own_block = tsend[rows(4 * y + x, 96)].astype(F32)
-    for at in range(15):
-        own_block += trecv[at].astype(F32)
-    zbuf[z] = own_block.astype(BF16)
-    step_rows = 96 // SUBS
-    ring = {}
-
-    def ring_send(step, way, part):
-        origin = lax.rem(z + 16 + (-(step - 1) if way == 0 else step - 1), 16)
-        ref = zbuf.at[origin, pl.ds(part * step_rows, step_rows)]
-        ring[step, way, part] = send(ref, ref, z_s.at[step, way, part], z_r.at[step, way, part], ups[way])
-
-    def parts(step, way):
-        if step < 8:
-            return range(SUBS)
-        return range(SUBS // 2) if way == 0 else range(SUBS // 2, SUBS)
-
-    for part in range(SUBS):
-        for way in range(2):
-            ring_send(1, way, part)
+    group_sum = near_in[0].astype(F32)
+    for at in range(1, 4):
+        group_sum += near_in[at].astype(F32)
+    far[zq] = group_sum.astype(BF16)
+    met(2)
+    far_copies = []
+    for j in range(1, 4):
+        to = lax.rem(zq + j, 4)
+        far_copies.append(
+            send(far.at[zq], far.at[zq], far_s.at[j], far_r.at[j], place(x, y, 4 * to + zr, c))
+        )
+    sent += far_copies
 
     @pl.when(chip == 0)
     def _():
@@ -310,13 +335,6 @@
     @pl.when(chip > 0)
     def _():
         row_down.wait_recv()
-
-    def ring_step(step):
-        for part in range(SUBS):
-            for way in range(2):
-                ring[step - 1, way, part].wait_recv()
-                if part in parts(step, way):
-                    ring_send(step, way, part)
 
     for row in range(3):
         for f in range(2):
@@ -333,17 +351,12 @@
         po[0, kind] = value[:160]
         po[1, kind] = value[160:]
 
-    ring_step(2)
     put(0, dot(cur, tap(0, 0), 1, 1) + dot(cur_s, tap(0, 2), 1, 1) + dot(prev, tap(2, 0), 1, 1) + dot(prev_s, tap(2, 2), 1, 1))
-    ring_step(3)
     put(1, dot(cur, tap(0, 1), 1, 1) + dot(prev, tap(2, 1), 1, 1))
-    ring_step(4)
     put(2, dot(cur, tap(1, 0), 1, 1) + dot(cur_s, tap(1, 2), 1, 1))
     put(3, dot(cur, tap(1, 1), 1, 1))
     pair_o = send(po.at[other], po_in, pair_s.at[6], pair_r.at[6], partner)
     sent.append(pair_o)
-    ring_step(5)
-    pair_o.wait_recv()
 
     def finish(f, r):
         block = pl.ds(f * 80, 80)
@@ -354,55 +367,47 @@
                 wide[lane, pl.ds(odd, 80, 2), :] = po[c, kind, block, across] + po_in[kind, block, across]
             outv[f, r, :, across] = wide[lane].astype(BF16)
 
-    finish(0, 0)
-    finish(0, 1)
-    ring_step(6)
-    finish(1, 0)
-    finish(1, 1)
-    write_out = pltpu.make_async_copy(outv, out_hbm, loc_sem.at[4])
-    write_out.start()
-    ring_step(7)
-    ring_step(8)
-    for way in range(2):
-        for part in parts(8, way):
-            ring[8, way, part].wait_recv()
-    sent += list(ring.values())
-    total = zbuf[0].astype(F32)
-    for at in range(1, 16):
-        total += zbuf[at].astype(F32)
-    fin[...] = total
-
-    far = pltpu.make_async_remote_copy(
-        src_ref=fin, dst_ref=fout.at[c], send_sem=fin_s.at[0], recv_sem=fin_r.at[c], device_id=final_to, device_id_type=MESH
+    for copy in far_copies:
+        copy.wait_recv()
+    quarter = far[0].astype(F32)
+    for at in range(1, 4):
+        quarter += far[at].astype(F32)
+    quad[...] = quarter
+    fin_copies = []
+    for flip in range(2):
+        for j in range(4):
+            if flip or j:
+                to = place(jnp.bitwise_xor(x, flip), y, 4 * zq + lax.rem(zr + j, 4), xl)
+                fin_copies.append(send(quad, fout.at[c, zr], fin_s.at[flip, j], fin_r.at[c, zr], to))
+    here = pltpu.make_async_copy(quad, fout.at[c, zr], fin_r.at[c, zr])
+    beside = pltpu.make_async_remote_copy(
+        src_ref=quad, dst_ref=fout.at[c, zr], send_sem=fin_s.at[0, 0], recv_sem=fin_r.at[c, zr], device_id=partner, device_id_type=MESH
     )
-    near = pltpu.make_async_remote_copy(
-        src_ref=fin, dst_ref=fout.at[c], send_sem=fin_s.at[1], recv_sem=fin_r.at[c], device_id=partner, device_id_type=MESH
-    )
-    far.start()
-
-    def landed(h):
-        pltpu.make_async_copy(fout.at[h], fout.at[h], fin_r.at[h]).wait()
 
     @pl.when(c == xl)
     def _():
-        fout[c] = fin[...]
-        landed(other)
+        here.start()
 
     @pl.when(c != xl)
     def _():
-        near.start()
-        landed(0)
-        landed(1)
-        near.wait_send()
-
-    writes = [
-        pltpu.make_async_copy(fout.at[h], gt_hbm.at[:, pl.ds(256 * h, 256)], loc_sem.at[5 + h]) for h in range(2)
-    ]
-    for copy in writes:
-        copy.start()
-    far.wait_send()
-    for copy in sent:
+        beside.start()
+
+    pair_o.wait_recv()
+    for f in range(2):
+        for r in range(2):
+            finish(f, r)
+
+    for h in range(2):
+        for q in range(4):
+            pltpu.make_async_copy(fout.at[h, q], fout.at[h, q], fin_r.at[h, q]).wait()
+            gt[pl.ds(48 * (q // 2), 48), pl.ds(256 * h + 128 * (q % 2), 128)] = fout[h, q]
+
+    for copy in sent + fin_copies:
         copy.wait_send()
+
+    @pl.when(c != xl)
+    def _():
+        beside.wait_send()
 
     @pl.when(tm > 0)
     def _():
@@ -416,10 +421,6 @@
     @pl.when(chip < 7)
     def _():
         row_down.wait_send()
-
-    write_out.wait()
-    for copy in writes:
-        copy.wait()
 
 
 def local(latents, grad_out, w_spatial, w_temporal):
@@ -432,7 +433,7 @@
             jax.ShapeDtypeStruct((96, 512), F32),
         ),
         in_specs=[pl.BlockSpec(memory_space=pl.ANY)] * 4,
-        out_specs=[pl.BlockSpec(memory_space=pl.ANY)] * 2,
+        out_specs=[pl.BlockSpec(memory_space=pltpu.VMEM)] * 2,
         scratch_shapes=[
             vmem((2, 2, 160, 256), BF16),
             vmem((2304, 256), BF16),
@@ -445,17 +446,18 @@
             vmem((1536, 256), F32),
             vmem((1536, 256), BF16),
             vmem((15, 96, 256), BF16),
-            vmem((16, 96, 256), BF16),
-            vmem((96, 256), F32),
-            vmem((2, 96, 256), F32),
+            vmem((4, 48, 128), BF16),
+            vmem((4, 48, 128), BF16),
+            vmem((4, 48, 128), BF16),
+            vmem((48, 128), F32),
+            vmem((2, 4, 48, 128), F32),
             vmem((2, 320, 256), F32),
             vmem((320, 256), F32),
             vmem((3, 2, 80, 256), BF16),
             vmem((3, 2, 80, 256), BF16),
             vmem((2, 4, 160, 256), F32),
             vmem((4, 160, 256), F32),
-            vmem((2, 2, 160, 256), BF16),
-            dma((7,)),
+            dma((4,)),
             dma((7,)),
             dma((7,)),
             dma((2, 8)),
@@ -466,13 +468,16 @@
             dma((4,)),
             dma((15,)),
             dma((15,)),
-            dma((9, 2, SUBS)),
-            dma((9, 2, SUBS)),
-            dma((2,)),
-            dma((2,)),
+            dma((4,)),
+            dma((4,)),
+            dma((4,)),
+            dma((4,)),
+            dma((2, 4)),
+            dma((2, 4)),
+            pltpu.SemaphoreType.REGULAR((3,)),
         ],
         compiler_params=pltpu.CompilerParams(
-            collective_id=0, has_side_effects=True, vmem_limit_bytes=48 * 2**20
+            collective_id=0, has_side_effects=True, vmem_limit_bytes=60 * 2**20
         ),
     )(latents, grad_out, w_spatial, w_temporal)
 

time: 86.3 us -> 71.3 us (0.83)
  Pallas kernels: 80.3 us -> 68.1 us
  local copies, waits for them, and re-layouts: 5.09 us -> 2.44 us
    pallas_call x1, Pallas kernels: 80.3 us -> 68.1 us  [local(): pl.pallas_call(kernel, out_shape=(jax.ShapeDtypeStruct(latents.shape, BF1...]
    unnamed x10 -> x4, local copies, waits for them, and re-layouts: 5.09 us -> 2.44 us
where the time goes in v2:
time: 71.3 us; the launch traced here: 71.2 us
  Pallas kernels  68.1 us (96%)
  local copies, waits for them, and re-layouts  2.44 us (3%)
    pallas_call x1, Pallas kernels, local(): pl.pallas_call(kernel, out_shape=(jax.ShapeDtypeStruct(latents.shape, BF1...  68.1 us
    unnamed x4, local copies, waits for them, and re-layouts  2.44 us

profile of v2, /device:TPU:1, one launch (start us, length us, event | category | flops | bytes accessed | tf_op | source)
XLA Modules:
  0.0 71.2 jit_solution(16629903732029946438)
XLA Ops:
  0.6 68.1 %shard_map.59 = (bf16[2,2,160,256]{3,2,1,0:T(8,128)(2,1)}, f32[96,512]{1,0:T(8,128)}) custom-call(bf16[2,2,160,256]{3,2,1,0:T(8,128)(2,1)} %lat_hbm.1, bf16[2,1,80,512]{3,2,1,0:T(8,128)(2,1)} %gout_hbm.1, bf16[144,512]{1,0:T(8,128)(2,1)} %ws_hbm.1, bf16[96,512]{1,0:T(8,128)(2,1)} %wt_hbm.1), custom_call_target="tpu_custom_call" | custom-call | tf_op jit(solution)/shard_map/pallas_call | solution.py:429
  68.7 0.0 copy-start
  68.8 1.8 %copy.8 = bf16[2,2,160,256]{3,2,1,0:T(8,128)(2,1)} copy(bf16[2,2,160,256]{3,2,1,0:T(8,128)(2,1)} %get-tuple-element.4) | data formatting | bytes 655360
  70.5 0.0 copy-done
  70.5 0.7 copy.9
Async XLA Ops:
  68.7 1.8 %copy-start = (f32[96,512]{1,0:T(8,128)S(1)}, f32[96,512]{1,0:T(8,128)}, u32[]{:S(2)}) copy-start(f32[96,512]{1,0:T(8,128)} %get-tuple-element.5) | copy-start | bytes 589828

commit v3 on v2

--- a/solution.py
+++ b/solution.py
@@ -8,8 +8,8 @@
 MESH = pl.DeviceIdType.MESH
 F32 = jnp.float32
 BF16 = jnp.bfloat16
-ARRIVAL = (4, 1, 3, 5, 7, 2, 6)
-RELAY = {4: 0, 1: 1, 3: 2, 5: 0, 7: 1, 2: 2, 6: 0}
+FAR = (2, 5, 7, 6)
+NEAR = (4, 1, 3)
 
 
 def dot(a, b, ca, cb):
@@ -23,7 +23,7 @@
 def kernel(
     lat_hbm, gout_hbm, ws_hbm, wt_hbm, outv, gt,
     lat, ws, wt, grads, eo, wide, patches, acts, tsum, tsend, trecv,
-    near, near_in, far, quad, fout, gap, gap_in, ga, shifted, po, po_in,
+    ws_other, wt_other, g_other, near, near_in, far, quad, fout, gap, gap_in, ga, shifted, po, po_in,
     loc_sem, pair_s, pair_r, ext_s, ext_r, rel_s, rel_r, halo_s, halo_r,
     rs_s, rs_r, near_s, near_r, far_s, far_r, fin_s, fin_r, known,
 ):
@@ -57,9 +57,12 @@
         pltpu.make_async_copy(wt_hbm.at[:, half(c)], wt.at[rows(sp, 96)], loc_sem.at[1]),
         pltpu.make_async_copy(lat_hbm, lat, loc_sem.at[2]),
         pltpu.make_async_copy(gout_hbm.at[:, 0, :, half(c)], grads.at[pl.ds(0, 2), c], loc_sem.at[3]),
+        pltpu.make_async_copy(ws_hbm.at[:, half(other)], ws_other, loc_sem.at[4]),
+        pltpu.make_async_copy(wt_hbm.at[:, half(other)], wt_other, loc_sem.at[5]),
+        pltpu.make_async_copy(gout_hbm.at[:, 0, :, half(other)], g_other, loc_sem.at[6]),
     ]
-    for copy in loads:
-        copy.start()
+    for at in (4, 0, 2, 5, 1, 6, 3):
+        loads[at].start()
 
     barrier = pltpu.get_barrier_semaphore()
     greeted = [partner, ups[0], ups[1], place(jnp.bitwise_xor(x, 1), y, z, other), (tm_next, sp), (tm_next, chip * 2 + other)]
@@ -86,12 +89,10 @@
         copy.start()
         return copy
 
-    pair_ws = send(ws_hbm.at[:, half(other)], ws.at[rows(sp, 144)], pair_s.at[0], pair_r.at[0], partner)
-    pair_wt = send(wt_hbm.at[:, half(other)], wt.at[rows(sp, 96)], pair_s.at[1], pair_r.at[1], partner)
-    pair_g = send(
-        gout_hbm.at[:, 0, :, half(other)], grads.at[pl.ds(0, 2), c], pair_s.at[2], pair_r.at[2], partner
-    )
-    sent += [pair_ws, pair_wt, pair_g]
+    loads[4].wait()
+    pair_ws = send(ws_other, ws.at[rows(sp, 144)], pair_s.at[0], pair_r.at[0], partner)
+    loads[5].wait()
+    pair_wt = send(wt_other, wt.at[rows(sp, 96)], pair_s.at[1], pair_r.at[1], partner)
 
     def piece_chip(r):
         dxo, dy = r // 4, r % 4
@@ -102,20 +103,54 @@
         tx = 3 - x if dxo else x
         return place(tx, lax.rem(y + dy, 4), z, c)
 
-    mine = chip * 2 + par
-    weights = ((ws, 144, 0), (wt, 96, 1))
-
-    def ext_send(which):
-        buf, count, lane = weights[which]
+    weights = ((ws, 144), (wt, 96))
+
+    def piece(which, index, part=None):
+        buf, count = weights[which]
+        if part is None:
+            return buf.at[rows(index, count)]
+        third = count // 3
+        return buf.at[pl.ds(pl.multiple_of(index * count + part * third, third), third)]
+
+    def ext_copies(which, group):
+        jobs = [(r, r) for r in FAR + NEAR] if group == 0 else [(r, 8 + at) for at, r in enumerate(NEAR)]
+        ref = piece(which, chip * 2 + (par if group == 0 else 1 - par))
         return [
-            send(buf.at[rows(mine, count)], buf.at[rows(mine, count)], ext_s.at[lane, r], ext_r.at[lane, r], ext_device(r))
-            for r in ARRIVAL
+            pltpu.make_async_remote_copy(
+                src_ref=ref,
+                dst_ref=ref,
+                send_sem=ext_s.at[which, slot],
+                recv_sem=ext_r.at[which, slot],
+                device_id=ext_device(r),
+                device_id_type=MESH,
+            )
+            for r, slot in jobs
         ]
 
+    ext = [[ext_copies(which, group) for group in range(2)] for which in range(2)]
+    for which in range(2):
+        for group in range(2):
+            sent += ext[which][group]
     loads[0].wait()
+
+    @pl.when(c == par)
+    def _():
+        for copy in ext[0][0]:
+            copy.start()
+
     pair_ws.wait_recv()
-    ext_ws = ext_send(0)
-    sent += ext_ws
+
+    @pl.when(c != par)
+    def _():
+        for copy in ext[0][0]:
+            copy.start()
+
+    for copy in ext[0][1]:
+        copy.start()
+
+    loads[6].wait()
+    pair_g = send(g_other, grads.at[pl.ds(0, 2), c], pair_s.at[2], pair_r.at[2], partner)
+    sent += [pair_ws, pair_wt, pair_g]
 
     halo = []
     for h in range(2):
@@ -194,22 +229,34 @@
     met(1)
     meet(2)
 
-    def relay(which, arriving):
-        buf, count, lane = weights[which]
-        copies = []
-        for at, r in enumerate(ARRIVAL):
-            arriving[at].wait_recv()
+    def relay(which):
+        for at, r in enumerate(FAR):
+            ext[which][0][at].wait_recv()
             index = piece_chip(r) * 2 + par
-            copies.append(
-                send(buf.at[rows(index, count)], buf.at[rows(index, count)], rel_s.at[lane, r], rel_r.at[lane, r], ups[RELAY[r]])
-            )
-        return copies
-
-    rel_ws = relay(0, ext_ws)
+            for part in range(3):
+                ref = piece(which, index, part) if at == 3 else piece(which, index)
+                if at == 3 or part == at:
+                    slot = 3 + part if at == 3 else at
+                    sent.append(send(ref, ref, rel_s.at[which, slot], rel_r.at[which, slot], ups[part]))
+
+    def all_here(which):
+        for copy in ext[which][0][4:] + ext[which][1]:
+            copy.wait_recv()
+        for at, r in enumerate(FAR):
+            index = piece_chip(r) * 2 + 1 - par
+            if at < 3:
+                ref = piece(which, index)
+                pltpu.make_async_copy(ref, ref, rel_r.at[which, at]).wait()
+            else:
+                for part in range(3):
+                    ref = piece(which, index, part)
+                    pltpu.make_async_copy(ref, ref, rel_r.at[which, 3 + part]).wait()
+
+    relay(0)
     loads[1].wait()
     pair_wt.wait_recv()
-    ext_wt = ext_send(1)
-    sent += rel_ws + ext_wt
+    for copy in ext[1][0] + ext[1][1]:
+        copy.start()
 
     @pl.when(chip < 7)
     def _():
@@ -217,12 +264,12 @@
 
     for f in range(2):
         place_patch(f, 1, 2)
-    for copy in rel_ws:
-        copy.wait_recv()
+    all_here(0)
 
     acts[c] = jnp.dot(patches[...], ws[...], preferred_element_type=F32).astype(BF16)
     pair_a = send(acts.at[c], acts.at[c], pair_s.at[4], pair_r.at[4], partner)
     sent.append(pair_a)
+    relay(1)
 
     loads[3].wait()
     pair_g.wait_recv()
@@ -258,10 +305,7 @@
         )
     sent += spread
 
-    rel_wt = relay(1, ext_wt)
-    sent += rel_wt
-    for copy in rel_wt:
-        copy.wait_recv()
+    all_here(1)
     for h in range(2):
         total = dot(frames(2, 2), wt[pl.ds(h * 256, 256)], 1, 1)
         total += dot(frames(1, 2), wt[pl.ds(512 + h * 256, 256)], 1, 1)
@@ -278,6 +322,24 @@
 
     pair_p = send(gap.at[other], gap_in, pair_s.at[5], pair_r.at[5], partner)
     sent.append(pair_p)
+
+    pair_p.wait_recv()
+    for f in range(2):
+        for i in range(2):
+            block = pl.ds((f * 2 + i) * 80, 80)
+            ga[1 + i, f] = (gap[c, block] + gap_in[block]).astype(BF16)
+    row_down = pltpu.make_async_remote_copy(
+        src_ref=ga.at[2],
+        dst_ref=ga.at[0],
+        send_sem=halo_s.at[3],
+        recv_sem=halo_r.at[3],
+        device_id=(tm, next_chip * 2 + c),
+        device_id_type=MESH,
+    )
+
+    @pl.when(chip < 7)
+    def _():
+        row_down.start()
 
     for copy in spread:
         copy.wait_recv()
@@ -295,23 +357,35 @@
     sent += near_copies
     near_in[zr] = near[zr]
 
-    pair_p.wait_recv()
-    for f in range(2):
-        for i in range(2):
-            block = pl.ds((f * 2 + i) * 80, 80)
-            ga[1 + i, f] = (gap[c, block] + gap_in[block]).astype(BF16)
-    row_down = pltpu.make_async_remote_copy(
-        src_ref=ga.at[2],
-        dst_ref=ga.at[0],
-        send_sem=halo_s.at[3],
-        recv_sem=halo_r.at[3],
-        device_id=(tm, next_chip * 2 + c),
-        device_id_type=MESH,
-    )
-
-    @pl.when(chip < 7)
-    def _():
-        row_down.start()
+    @pl.when(chip == 0)
+    def _():
+        ga[0] = jnp.zeros_like(ga[0])
+
+    @pl.when(chip > 0)
+    def _():
+        row_down.wait_recv()
+
+    for row in range(3):
+        for f in range(2):
+            moved = jnp.where(first, 0.0, pltpu.roll(ga[row, f].astype(F32), 1, 0))
+            shifted[row, f] = moved.astype(BF16)
+
+    def tap(r, s):
+        return ws[pl.ds((3 * r + s) * 256, 256)]
+
+    cur, prev = ga[1:3].reshape(320, 256), ga[0:2].reshape(320, 256)
+    cur_s, prev_s = shifted[1:3].reshape(320, 256), shifted[0:2].reshape(320, 256)
+
+    def put(kind, value):
+        po[0, kind] = value[:160]
+        po[1, kind] = value[160:]
+
+    put(0, dot(cur, tap(0, 0), 1, 1) + dot(cur_s, tap(0, 2), 1, 1) + dot(prev, tap(2, 0), 1, 1) + dot(prev_s, tap(2, 2), 1, 1))
+    put(1, dot(cur, tap(0, 1), 1, 1) + dot(prev, tap(2, 1), 1, 1))
+    put(2, dot(cur, tap(1, 0), 1, 1) + dot(cur_s, tap(1, 2), 1, 1))
+    put(3, dot(cur, tap(1, 1), 1, 1))
+    pair_o = send(po.at[other], po_in, pair_s.at[6], pair_r.at[6], partner)
+    sent.append(pair_o)
 
     for copy in near_copies:
         copy.wait_recv()
@@ -328,36 +402,6 @@
         )
     sent += far_copies
 
-    @pl.when(chip == 0)
-    def _():
-        ga[0] = jnp.zeros_like(ga[0])
-
-    @pl.when(chip > 0)
-    def _():
-        row_down.wait_recv()
-
-    for row in range(3):
-        for f in range(2):
-            moved = jnp.where(first, 0.0, pltpu.roll(ga[row, f].astype(F32), 1, 0))
-            shifted[row, f] = moved.astype(BF16)
-
-    def tap(r, s):
-        return ws[pl.ds((3 * r + s) * 256, 256)]
-
-    cur, prev = ga[1:3].reshape(320, 256), ga[0:2].reshape(320, 256)
-    cur_s, prev_s = shifted[1:3].reshape(320, 256), shifted[0:2].reshape(320, 256)
-
-    def put(kind, value):
-        po[0, kind] = value[:160]
-        po[1, kind] = value[160:]
-
-    put(0, dot(cur, tap(0, 0), 1, 1) + dot(cur_s, tap(0, 2), 1, 1) + dot(prev, tap(2, 0), 1, 1) + dot(prev_s, tap(2, 2), 1, 1))
-    put(1, dot(cur, tap(0, 1), 1, 1) + dot(prev, tap(2, 1), 1, 1))
-    put(2, dot(cur, tap(1, 0), 1, 1) + dot(cur_s, tap(1, 2), 1, 1))
-    put(3, dot(cur, tap(1, 1), 1, 1))
-    pair_o = send(po.at[other], po_in, pair_s.at[6], pair_r.at[6], partner)
-    sent.append(pair_o)
-
     def finish(f, r):
         block = pl.ds(f * 80, 80)
         for lane in range(2):
@@ -367,12 +411,17 @@
                 wide[lane, pl.ds(odd, 80, 2), :] = po[c, kind, block, across] + po_in[kind, block, across]
             outv[f, r, :, across] = wide[lane].astype(BF16)
 
+    pair_o.wait_recv()
+    for f in range(2):
+        for r in range(2):
+            finish(f, r)
+
     for copy in far_copies:
         copy.wait_recv()
     quarter = far[0].astype(F32)
     for at in range(1, 4):
         quarter += far[at].astype(F32)
-    quad[...] = quarter
+    quad[...] = quarter.astype(BF16)
     fin_copies = []
     for flip in range(2):
         for j in range(4):
@@ -392,15 +441,10 @@
     def _():
         beside.start()
 
-    pair_o.wait_recv()
-    for f in range(2):
-        for r in range(2):
-            finish(f, r)
-
     for h in range(2):
         for q in range(4):
             pltpu.make_async_copy(fout.at[h, q], fout.at[h, q], fin_r.at[h, q]).wait()
-            gt[pl.ds(48 * (q // 2), 48), pl.ds(256 * h + 128 * (q % 2), 128)] = fout[h, q]
+            gt[pl.ds(48 * (q // 2), 48), pl.ds(256 * h + 128 * (q % 2), 128)] = fout[h, q].astype(F32)
 
     for copy in sent + fin_copies:
         copy.wait_send()
@@ -446,24 +490,27 @@
             vmem((1536, 256), F32),
             vmem((1536, 256), BF16),
             vmem((15, 96, 256), BF16),
+            vmem((144, 256), BF16),
+            vmem((96, 256), BF16),
+            vmem((2, 80, 256), BF16),
             vmem((4, 48, 128), BF16),
             vmem((4, 48, 128), BF16),
             vmem((4, 48, 128), BF16),
-            vmem((48, 128), F32),
-            vmem((2, 4, 48, 128), F32),
+            vmem((48, 128), BF16),
+            vmem((2, 4, 48, 128), BF16),
             vmem((2, 320, 256), F32),
             vmem((320, 256), F32),
             vmem((3, 2, 80, 256), BF16),
             vmem((3, 2, 80, 256), BF16),
             vmem((2, 4, 160, 256), F32),
             vmem((4, 160, 256), F32),
-            dma((4,)),
             dma((7,)),
             dma((7,)),
-            dma((2, 8)),
-            dma((2, 8)),
-            dma((2, 8)),
-            dma((2, 8)),
+            dma((7,)),
+            dma((2, 11)),
+            dma((2, 11)),
+            dma((2, 6)),
+            dma((2, 6)),
             dma((4,)),
             dma((4,)),
             dma((15,)),

time: 71.3 us -> 68.9 us (0.966); the launches traced: 71.2 us -> 67.6 us
  Pallas kernels: 68.1 us -> 64.6 us
    pallas_call x1, Pallas kernels: 68.1 us -> 64.6 us  [local(): pl.pallas_call(kernel, out_shape=(jax.ShapeDtypeStruct(latents.shape, BF1...]
where the time goes in v3:
time: 68.9 us; the launch traced here: 67.6 us
  Pallas kernels  64.6 us (94%)
  local copies, waits for them, and re-layouts  2.44 us (4%)
    pallas_call x1, Pallas kernels, local(): pl.pallas_call(kernel, out_shape=(jax.ShapeDtypeStruct(latents.shape, BF1...  64.6 us
    unnamed x4, local copies, waits for them, and re-layouts  2.44 us

profile of v3, /device:TPU:1, one launch (start us, length us, event | category | flops | bytes accessed | tf_op | source)
XLA Modules:
  0.0 67.6 jit_solution(8994353428430273107)
XLA Ops:
  0.6 64.6 %shard_map.59 = (bf16[2,2,160,256]{3,2,1,0:T(8,128)(2,1)}, f32[96,512]{1,0:T(8,128)}) custom-call(bf16[2,2,160,256]{3,2,1,0:T(8,128)(2,1)} %lat_hbm.1, bf16[2,1,80,512]{3,2,1,0:T(8,128)(2,1)} %gout_hbm.1, bf16[144,512]{1,0:T(8,128)(2,1)} %ws_hbm.1, bf16[96,512]{1,0:T(8,128)(2,1)} %wt_hbm.1), custom_call_target="tpu_custom_call" | custom-call | tf_op jit(solution)/shard_map/pallas_call | solution.py:473
  65.2 0.0 copy-start
  65.2 1.8 %copy.8 = bf16[2,2,160,256]{3,2,1,0:T(8,128)(2,1)} copy(bf16[2,2,160,256]{3,2,1,0:T(8,128)(2,1)} %get-tuple-element.4) | data formatting | bytes 655360
  67.0 0.0 copy-done
  67.0 0.7 %copy.9 = f32[96,512]{1,0:T(8,128)} copy(f32[96,512]{1,0:T(8,128)S(1)} %copy-done) | data formatting | bytes 393216
Async XLA Ops:
  65.2 1.8 %copy-start = (f32[96,512]{1,0:T(8,128)S(1)}, f32[96,512]{1,0:T(8,128)}, u32[]{:S(2)}) copy-start(f32[96,512]{1,0:T(8,128)} %get-tuple-element.5) | copy-start | bytes 589828

commit v4 on v3

--- a/solution.py
+++ b/solution.py
@@ -52,6 +52,13 @@
     def rows(index, count):
         return pl.ds(pl.multiple_of(index * count, count), count)
 
+    def ext_device(r):
+        dxo, dy = r // 4, r % 4
+        tx = 3 - x if dxo else x
+        return place(tx, lax.rem(y + dy, 4), z, c)
+
+    prev_chip = lax.rem(chip + 7, 8)
+    next_chip = lax.rem(chip + 1, 8)
     loads = [
         pltpu.make_async_copy(ws_hbm.at[:, half(c)], ws.at[rows(sp, 144)], loc_sem.at[0]),
         pltpu.make_async_copy(wt_hbm.at[:, half(c)], wt.at[rows(sp, 96)], loc_sem.at[1]),
@@ -65,8 +72,9 @@
         loads[at].start()
 
     barrier = pltpu.get_barrier_semaphore()
-    greeted = [partner, ups[0], ups[1], place(jnp.bitwise_xor(x, 1), y, z, other), (tm_next, sp), (tm_next, chip * 2 + other)]
-    greeted += [place(px, py, z, c) for px, py in plane]
+    xs = jnp.bitwise_xor(x, 1)
+    greeted = [partner, *ups, place(xs, y, z, other), (tm_next, sp), (tm_next, chip * 2 + other)]
+    greeted += [(tm, next_chip * 2 + c)] + [ext_device(r) for r in range(1, 8)]
     for device in greeted:
         pl.semaphore_signal(barrier, inc=1, device_id=device, device_id_type=MESH)
     pl.semaphore_wait(barrier, len(greeted))
@@ -97,11 +105,6 @@
     def piece_chip(r):
         dxo, dy = r // 4, r % 4
         return lax.rem(y + 4 - dy, 4) * 2 + jnp.bitwise_xor(xh, dxo)
-
-    def ext_device(r):
-        dxo, dy = r // 4, r % 4
-        tx = 3 - x if dxo else x
-        return place(tx, lax.rem(y + dy, 4), z, c)
 
     weights = ((ws, 144), (wt, 96))
 
@@ -133,20 +136,17 @@
             sent += ext[which][group]
     loads[0].wait()
 
-    @pl.when(c == par)
-    def _():
-        for copy in ext[0][0]:
-            copy.start()
-
+    def start_ext(condition, group):
+        @pl.when(condition)
+        def _():
+            for copy in ext[0][group]:
+                copy.start()
+
+    start_ext(c == par, 0)
+    start_ext(c != par, 1)
     pair_ws.wait_recv()
-
-    @pl.when(c != par)
-    def _():
-        for copy in ext[0][0]:
-            copy.start()
-
-    for copy in ext[0][1]:
-        copy.start()
+    start_ext(c != par, 0)
+    start_ext(c == par, 1)
 
     loads[6].wait()
     pair_g = send(g_other, grads.at[pl.ds(0, 2), c], pair_s.at[2], pair_r.at[2], partner)
@@ -185,11 +185,9 @@
     sent.append(pair_eo)
     pair_eo.wait_recv()
 
-    prev_chip = lax.rem(chip + 7, 8)
-    next_chip = lax.rem(chip + 1, 8)
     row_up = pltpu.make_async_remote_copy(
-        src_ref=eo.at[0],
-        dst_ref=eo.at[4],
+        src_ref=eo.at[0, c],
+        dst_ref=eo.at[4, c],
         send_sem=halo_s.at[2],
         recv_sem=halo_r.at[2],
         device_id=(tm, prev_chip * 2 + c),
@@ -252,7 +250,22 @@
                     ref = piece(which, index, part)
                     pltpu.make_async_copy(ref, ref, rel_r.at[which, 3 + part]).wait()
 
+    row_pair = pltpu.make_async_remote_copy(
+        src_ref=eo.at[4, c],
+        dst_ref=eo.at[4, c],
+        send_sem=pair_s.at[7],
+        recv_sem=pair_r.at[7],
+        device_id=partner,
+        device_id_type=MESH,
+    )
+
     relay(0)
+
+    @pl.when(chip < 7)
+    def _():
+        row_up.wait_recv()
+        row_pair.start()
+
     loads[1].wait()
     pair_wt.wait_recv()
     for copy in ext[1][0] + ext[1][1]:
@@ -260,7 +273,7 @@
 
     @pl.when(chip < 7)
     def _():
-        row_up.wait_recv()
+        row_pair.wait_recv()
 
     for f in range(2):
         place_patch(f, 1, 2)
@@ -269,7 +282,6 @@
     acts[c] = jnp.dot(patches[...], ws[...], preferred_element_type=F32).astype(BF16)
     pair_a = send(acts.at[c], acts.at[c], pair_s.at[4], pair_r.at[4], partner)
     sent.append(pair_a)
-    relay(1)
 
     loads[3].wait()
     pair_g.wait_recv()
@@ -305,6 +317,7 @@
         )
     sent += spread
 
+    relay(1)
     all_here(1)
     for h in range(2):
         total = dot(frames(2, 2), wt[pl.ds(h * 256, 256)], 1, 1)
@@ -464,6 +477,10 @@
 
     @pl.when(chip < 7)
     def _():
+        row_pair.wait_send()
+
+    @pl.when(chip < 7)
+    def _():
         row_down.wait_send()
 
 
@@ -473,11 +490,10 @@
     return pl.pallas_call(
         kernel,
         out_shape=(
-            jax.ShapeDtypeStruct(latents.shape, BF16),
-            jax.ShapeDtypeStruct((96, 512), F32),
+            pltpu.VMEM(latents.shape, BF16),
+            pltpu.VMEM((96, 512), F32),
         ),
         in_specs=[pl.BlockSpec(memory_space=pl.ANY)] * 4,
-        out_specs=[pl.BlockSpec(memory_space=pltpu.VMEM)] * 2,
         scratch_shapes=[
             vmem((2, 2, 160, 256), BF16),
             vmem((2304, 256), BF16),
@@ -505,8 +521,8 @@
             vmem((2, 4, 160, 256), F32),
             vmem((4, 160, 256), F32),
             dma((7,)),
-            dma((7,)),
-            dma((7,)),
+            dma((8,)),
+            dma((8,)),
             dma((2, 11)),
             dma((2, 11)),
             dma((2, 6)),

time: 68.9 us -> 65.5 us (0.951); the launches traced: 67.6 us -> 65.4 us
  Pallas kernels: 64.6 us -> 63.3 us
  local copies, waits for them, and re-layouts: 2.44 us -> 1.4 us
    pallas_call x1, Pallas kernels: 64.6 us -> 63.3 us  [local(): pl.pallas_call(kernel, out_shape=(pltpu.VMEM(latents.shape, BF16), pltpu....]
    unnamed x4 -> x2, local copies, waits for them, and re-layouts: 2.44 us -> 1.4 us
where the time goes in v4:
time: 65.5 us; the launch traced here: 65.4 us
  Pallas kernels  63.3 us (97%)
  local copies, waits for them, and re-layouts  1.4 us (2%)
    pallas_call x1, Pallas kernels, local(): pl.pallas_call(kernel, out_shape=(pltpu.VMEM(latents.shape, BF16), pltpu....  63.3 us
    unnamed x2, local copies, waits for them, and re-layouts  1.4 us

profile of v4, /device:TPU:1, one launch (start us, length us, event | category | flops | bytes accessed | tf_op | source)
XLA Modules:
  0.0 65.4 jit_solution(7492767092606003267)
XLA Ops:
  0.6 63.3 %shard_map.59 = (bf16[2,2,160,256]{3,2,1,0:T(8,128)(2,1)S(1)}, f32[96,512]{1,0:T(8,128)S(1)}) custom-call(bf16[2,2,160,256]{3,2,1,0:T(8,128)(2,1)} %lat_hbm.1, bf16[2,1,80,512]{3,2,1,0:T(8,128)(2,1)} %gout_hbm.1, bf16[144,512]{1,0:T(8,128)(2,1)} %ws_hbm.1, bf16[96,512]{1,0:T(8,128)(2,1)} %wt_hbm.1), custom_call_target="tpu_custom_call" | custom-call | tf_op jit(solution)/shard_map/pallas_call | solution.py:490
  64.0 0.7 %copy.8 = bf16[2,2,160,256]{3,2,1,0:T(8,128)(2,1)} copy(bf16[2,2,160,256]{3,2,1,0:T(8,128)(2,1)S(1)} %get-tuple-element.2) | data formatting | bytes 655360
  64.7 0.7 %copy.9 = f32[96,512]{1,0:T(8,128)} copy(f32[96,512]{1,0:T(8,128)S(1)} %get-tuple-element.3) | data formatting | bytes 393216

commit v5 on v4

--- a/solution.py
+++ b/solution.py
@@ -22,7 +22,7 @@
 
 def kernel(
     lat_hbm, gout_hbm, ws_hbm, wt_hbm, outv, gt,
-    lat, ws, wt, grads, eo, wide, patches, acts, tsum, tsend, trecv,
+    lat, ws, wt, grads, eo, wide, patches, acts, tsend, trecv,
     ws_other, wt_other, g_other, near, near_in, far, quad, fout, gap, gap_in, ga, shifted, po, po_in,
     loc_sem, pair_s, pair_r, ext_s, ext_r, rel_s, rel_r, halo_s, halo_r,
     rs_s, rs_r, near_s, near_r, far_s, far_r, fin_s, fin_r, known,
@@ -43,7 +43,8 @@
     for dy in range(4):
         for dx in range(4):
             if dx or dy:
-                plane.append((lax.rem(x + dx, 4), lax.rem(y + dy, 4)))
+                plane.append((min(dx, 4 - dx) + min(dy, 4 - dy), lax.rem(x + dx, 4), lax.rem(y + dy, 4)))
+    plane = [entry[1:] for entry in sorted(plane, key=lambda entry: -entry[0])]
     tm_next, tm_prev = lax.rem(tm + 1, 32), lax.rem(tm + 31, 32)
 
     def half(index):
@@ -296,19 +297,22 @@
     def frames(start, count):
         return grads[start : start + count].reshape(count * 160, 256)
 
-    for k in range(3):
-        for h in range(2):
-            tsum[pl.ds(k * 512 + h * 256, 256)] = dot(acts[h], frames(2 - k, 2), 0, 0)
+    def terms(starts):
+        for k in range(3):
+            for h in range(2):
+                value = dot(acts[h], frames(2 - k, 2), 0, 0)
+                for frame in range(2 - k if starts else 0):
+                    value += dot(acts[h, 0:160], frames(frame, 1), 0, 0)
+                tsend[pl.ds(k * 512 + h * 256, 256)] = value.astype(BF16)
+
+    @pl.when(tm > 0)
+    def _():
+        terms(False)
 
     @pl.when(tm == 0)
     def _():
-        for h in range(2):
-            first_acts = acts[h, 0:160]
-            zero = dot(first_acts, frames(0, 1), 0, 0)
-            tsum[pl.ds(h * 256, 256)] += zero + dot(first_acts, frames(1, 1), 0, 0)
-            tsum[pl.ds(512 + h * 256, 256)] += zero
-
-    tsend[...] = tsum[...].astype(BF16)
+        terms(True)
+
     spread = []
     for at, (px, py) in enumerate(plane):
         block = 4 * py + px
@@ -408,7 +412,7 @@
     far[zq] = group_sum.astype(BF16)
     met(2)
     far_copies = []
-    for j in range(1, 4):
+    for j in (2, 1, 3):
         to = lax.rem(zq + j, 4)
         far_copies.append(
             send(far.at[zq], far.at[zq], far_s.at[j], far_r.at[j], place(x, y, 4 * to + zr, c))
@@ -436,8 +440,8 @@
         quarter += far[at].astype(F32)
     quad[...] = quarter.astype(BF16)
     fin_copies = []
-    for flip in range(2):
-        for j in range(4):
+    for flip in (1, 0):
+        for j in (2, 3, 1, 0):
             if flip or j:
                 to = place(jnp.bitwise_xor(x, flip), y, 4 * zq + lax.rem(zr + j, 4), xl)
                 fin_copies.append(send(quad, fout.at[c, zr], fin_s.at[flip, j], fin_r.at[c, zr], to))
@@ -503,7 +507,6 @@
             vmem((2, 160, 128), F32),
             vmem((320, 2304), BF16),
             vmem((2, 320, 256), BF16),
-            vmem((1536, 256), F32),
             vmem((1536, 256), BF16),
             vmem((15, 96, 256), BF16),
             vmem((144, 256), BF16),

time: 65.5 us -> 64.6 us (0.986)
  Pallas kernels: 63.3 us -> 62.1 us
    pallas_call x1, Pallas kernels: 63.3 us -> 62.1 us  [local(): pl.pallas_call(kernel, out_shape=(pltpu.VMEM(latents.shape, BF16), pltpu....]
where the time goes in v5:
time: 64.6 us; the launch traced here: 64.1 us
  Pallas kernels  62.1 us (96%)
  local copies, waits for them, and re-layouts  1.4 us (2%)
    pallas_call x1, Pallas kernels, local(): pl.pallas_call(kernel, out_shape=(pltpu.VMEM(latents.shape, BF16), pltpu....  62.1 us
    unnamed x2, local copies, waits for them, and re-layouts  1.4 us

profile of v5, /device:TPU:1, one launch (start us, length us, event | category | flops | bytes accessed | tf_op | source)
XLA Modules:
  0.0 64.1 jit_solution(9145218634032473846)
XLA Ops:
  0.6 62.1 %shard_map.59 = (bf16[2,2,160,256]{3,2,1,0:T(8,128)(2,1)S(1)}, f32[96,512]{1,0:T(8,128)S(1)}) custom-call(bf16[2,2,160,256]{3,2,1,0:T(8,128)(2,1)} %lat_hbm.1, bf16[2,1,80,512]{3,2,1,0:T(8,128)(2,1)} %gout_hbm.1, bf16[144,512]{1,0:T(8,128)(2,1)} %ws_hbm.1, bf16[96,512]{1,0:T(8,128)(2,1)} %wt_hbm.1), custom_call_target="tpu_custom_call" | custom-call | tf_op jit(solution)/shard_map/pallas_call | solution.py:494
  62.7 0.7 %copy.8 = bf16[2,2,160,256]{3,2,1,0:T(8,128)(2,1)} copy(bf16[2,2,160,256]{3,2,1,0:T(8,128)(2,1)S(1)} %get-tuple-element.2) | data formatting | bytes 655360
  63.5 0.7 %copy.9 = f32[96,512]{1,0:T(8,128)} copy(f32[96,512]{1,0:T(8,128)S(1)} %get-tuple-element.3) | data formatting | bytes 393216
